TPU v7x, 256 devices: a whole 4x4x8 slice. The times are simulated.
256 devices in a mesh: frame: 64 (over x, y_hi, z), head: 4 (over y_lo, core).
Axes of the slice: x: 4, y: 4 (y_hi: 2, y_lo: 2; y = y_hi * 2 + y_lo), z: 8, core: 2. Of those that a mesh axis runs over, the one named last changes fastest.
Arguments:
- frames: bfloat16 [32768, 1536], P('frame'), may hold values from -24 to 24
- glu_weight: bfloat16 [2, 1536, 1536], P(None, None, 'head'), may hold values from -0.15625 to 0.15625
- depth_kernel: float32 [31, 1536], P(None, 'head'), may hold values from -1 to 1
- bn_scale: float32 [1536], P('head'), may hold values from 0.5 to 2
- bn_shift: float32 [1536], P('head'), may hold values from -2.5 to 2.5
- point_weight: bfloat16 [1536, 1536], P('head'), may hold values from -0.15625 to 0.15625
- qkv_weight: bfloat16 [3, 1536, 1536], P(None, None, 'head'), may hold values from -3 to 3
- out_weight: bfloat16 [1536, 1536], P('head'), may hold values from -0.15625 to 0.15625
Outputs:
- block_out: bfloat16 [32768, 1536], P('frame', 'head')
All inputs are finite; a program needn't handle non-finite values.
Results may differ from a plain program's by a relative error of at most 0.018.
Values may be sent and summed in bfloat16 or wider, within the bound.
A program may use at most 128 MiB of HBM per device.

v0:
```python
import functools

import jax
import jax.numpy as jnp
import numpy as np
from jax import lax
from jax.experimental import pallas as pl
from jax.experimental.pallas import tpu as pltpu
from jax.sharding import PartitionSpec as P

D = 1536
HD = 96
HALF_HD = HD // 2
KW = 31
HALF = 15
EDGE = 16
ROWS = 512
WIDTH = 384
QUARTER = 96
PIECE = 48
PART = 128
PARTS = ROWS // PART
SHARE = PART // 2
LANES = 128
CHUNK = 128
CHUNKS = ROWS // CHUNK
HEADS_HERE = 4
RING = 8
GROUP = 4
WINDOW = 9
UNIT = 2 * HD
PADDED_UNIT = UNIT + 16
SCALE = HD ** (-0.5) * 1.4426950408889634
MESH = pl.DeviceIdType.MESH
F32 = jnp.float32
BF16 = jnp.bfloat16


def contract(lhs, rhs, lhs_dim, rhs_dim):
    return lax.dot_general(
        lhs, rhs, (((lhs_dim,), (rhs_dim,)), ((), ())), preferred_element_type=F32
    )


def place(frame_count):
    frame = lax.axis_index("frame")
    head = lax.axis_index("head")
    ring, spot = frame // RING, frame % RING
    half, slot = spot // GROUP, spot % GROUP
    pair, core = head // 2, head % 2
    groups = frame_count // GROUP

    def partner(index):
        return (RING * ring + GROUP * core + index, 2 * pair + half)

    def is_self(index):
        return jnp.logical_and(core == half, slot == index)

    def group_device(by):
        group = (2 * ring + core + by + groups) % groups
        return (RING * (group // 2) + spot, 2 * pair + group % 2)

    def head_device(pair_flip, core_flip):
        to_pair = 1 - pair if pair_flip else pair
        to_core = 1 - core if core_flip else core
        return (frame, 2 * to_pair + to_core)

    def frame_device(by):
        return ((frame + by + frame_count) % frame_count, head)

    def spot_device(by):
        return (RING * ring + (spot + by + RING) % RING, head)

    def other_device():
        return (2 * RING * (ring // 2) + RING * (1 - ring % 2) + spot, 2 * (1 - pair) + core)

    return (
        partner,
        is_self,
        group_device,
        head_device,
        frame_device,
        spot_device,
        other_device,
        half,
        slot,
        core,
    )


def remote(source, target, send_sem, recv_sem, device):
    return pltpu.make_async_remote_copy(
        src_ref=source,
        dst_ref=target,
        send_sem=send_sem,
        recv_sem=recv_sem,
        device_id=device,
        device_id_type=MESH,
    )


def norm_rows(block):
    wide = block.astype(F32)
    center = wide - jnp.mean(wide, axis=-1, keepdims=True)
    spread = jnp.mean(center * center, axis=-1, keepdims=True)
    return (center * lax.rsqrt(spread + 1e-05)).astype(BF16)


def kernel(
    frame_count,
    frames_hbm,
    glu_hbm,
    depth_hbm,
    scale_hbm,
    shift_hbm,
    point_hbm,
    qkv_hbm,
    weight_hbm,
    angle_hbm,
    out_ref,
    frames,
    glu,
    point_all,
    key_value_weight,
    query_weight,
    weight_ref,
    angle,
    taps_ref,
    scale_ref,
    shift_ref,
    edges,
    normed,
    gated,
    swished,
    swished_all,
    sums,
    terms,
    residual,
    residual_send,
    normed_again,
    rotation,
    kv_ref,
    q_ref,
    kv_all,
    keys,
    q_all,
    scores,
    far_scores,
    peaks,
    totals,
    mixed,
    gathered,
    near_send,
    near_recv,
    far_own,
    far_send,
    far_recv,
    load_sem,
    edge_send_sem,
    edge_recv_sem,
    weight_y_send_sem,
    weight_y_recv_sem,
    weight_x_send_sem,
    weight_x_recv_sem,
    weight_near_send_sem,
    weight_near_recv_sem,
    swished_send_sem,
    swished_recv_sem,
    normed_send_sem,
    normed_recv_sem,
    residual_send_sem,
    residual_recv_sem,
    kv_send_sem,
    kv_recv_sem,
    q_send_sem,
    q_recv_sem,
    relay_send_sem,
    relay_recv_sem,
    o_send_sem,
    o_recv_sem,
    near_send_sem,
    near_recv_sem,
    far_send_sem,
    far_recv_sem,
):
    (
        partner,
        is_self,
        group_device,
        head_device,
        frame_device,
        spot_device,
        other_device,
        half,
        slot,
        core,
    ) = place(frame_count)
    frame = lax.axis_index("frame")
    own_head = lax.axis_index("head")
    pair = own_head // 2
    near_head = 2 * pair + 1 - core
    far_head = 2 * (1 - pair) + core
    cross_head = 2 * (1 - pair) + 1 - core

    def columns_of(head):
        return pl.ds(pl.multiple_of(head * WIDTH, 128), WIDTH)

    colour = (frame // (2 * RING) + frame % RING) % 4
    quarters = [colour, (colour + 2) % 4, (colour + 3) % 4, (colour + 1) % 4]

    def point_rows(head, start, size):
        return point_all.at[pl.ds(pl.multiple_of(head * WIDTH + start, 16), size)]

    loads = [
        pltpu.make_async_copy(point_hbm, point_rows(own_head, 0, WIDTH), load_sem.at[0]),
        pltpu.make_async_copy(frames_hbm, frames, load_sem.at[1]),
        pltpu.make_async_copy(glu_hbm.at[0], glu.at[:, pl.ds(0, WIDTH)], load_sem.at[2]),
        pltpu.make_async_copy(glu_hbm.at[1], glu.at[:, pl.ds(WIDTH, WIDTH)], load_sem.at[3]),
        pltpu.make_async_copy(depth_hbm, taps_ref, load_sem.at[4]),
        pltpu.make_async_copy(scale_hbm, scale_ref.at[0], load_sem.at[5]),
        pltpu.make_async_copy(shift_hbm, shift_ref.at[0], load_sem.at[6]),
        pltpu.make_async_copy(angle_hbm, angle, load_sem.at[7]),
        pltpu.make_async_copy(
            qkv_hbm.at[1], key_value_weight.at[:, pl.ds(0, WIDTH)], load_sem.at[8]
        ),
        pltpu.make_async_copy(
            qkv_hbm.at[2], key_value_weight.at[:, pl.ds(WIDTH, WIDTH)], load_sem.at[9]
        ),
        pltpu.make_async_copy(qkv_hbm.at[0], query_weight, load_sem.at[10]),
        pltpu.make_async_copy(weight_hbm, weight_ref, load_sem.at[11]),
    ]
    for load in loads[:7]:
        load.start()

    barrier = pltpu.get_barrier_semaphore()

    def greet(device):
        pl.semaphore_signal(barrier, inc=1, device_id=device, device_id_type=MESH)

    for index in range(GROUP):

        @pl.when(jnp.logical_not(is_self(index)))
        def _():
            greet(partner(index))

    greet(group_device(1))
    greet(group_device(-1))
    greet(head_device(False, True))
    greet(head_device(True, False))
    greet(head_device(True, True))
    greet(frame_device(1))
    greet(frame_device(-1))
    greet(frame_device(2 * RING))
    greet(frame_device(-2 * RING))
    greet(other_device())
    greet(spot_device(1))
    greet(spot_device(-1))
    pl.semaphore_wait(barrier, 16 - (core == half).astype(jnp.int32))

    def weight_y_copy(turn, side):
        block = point_rows(own_head, QUARTER * quarters[turn] + PIECE * side, PIECE)
        return remote(
            block,
            block,
            weight_y_send_sem.at[turn, side],
            weight_y_recv_sem.at[turn, side],
            other_device() if side else head_device(True, False),
        )

    def weight_y_arrival(turn, side):
        block = point_rows(far_head, QUARTER * quarters[turn] + PIECE * side, PIECE)
        return remote(
            block,
            block,
            weight_y_send_sem.at[turn, side],
            weight_y_recv_sem.at[turn, side],
            other_device() if side else head_device(True, False),
        )

    def weight_x_copy(way, side):
        block = point_rows(far_head, QUARTER * quarters[0] + PIECE * side, PIECE)
        return remote(
            block,
            block,
            weight_x_send_sem.at[way, side],
            weight_x_recv_sem.at[way, side],
            spot_device(-1 if way else 1) if side else frame_device(-2 * RING if way else 2 * RING),
        )

    def weight_x_arrival(way, side):
        block = point_rows(far_head, QUARTER * quarters[2 + way] + PIECE * side, PIECE)
        return remote(
            block,
            block,
            weight_x_send_sem.at[way, side],
            weight_x_recv_sem.at[way, side],
            spot_device(-1 if way else 1) if side else frame_device(-2 * RING if way else 2 * RING),
        )

    def weight_near_copy(index, arriving):
        if index == 0:
            block = point_rows(near_head if arriving else own_head, 0, WIDTH)
        else:
            block = point_rows(
                cross_head if arriving else far_head, QUARTER * quarters[index - 1], QUARTER
            )
        return remote(
            block,
            block,
            weight_near_send_sem.at[index],
            weight_near_recv_sem.at[index],
            head_device(False, True),
        )

    loads[0].wait()
    weight_y_copy(0, 0).start()
    weight_y_copy(0, 1).start()
    loads[1].wait()

    def edge_copy(side):
        rows = pl.ds(ROWS - EDGE, EDGE) if side == 0 else pl.ds(0, EDGE)
        return remote(
            frames.at[rows],
            edges.at[side],
            edge_send_sem.at[side],
            edge_recv_sem.at[side],
            frame_device(1 if side == 0 else -1),
        )

    edge_copy(0).start()
    edge_copy(1).start()

    def norm_block(index, carry):
        start = pl.multiple_of(index * 64, 64)
        normed[pl.ds(pl.multiple_of(start + EDGE, 16), 64)] = norm_rows(frames[pl.ds(start, 64)])
        return carry

    lax.fori_loop(0, ROWS // 64, norm_block, 0)
    weight_y_copy(1, 0).start()
    weight_y_copy(1, 1).start()
    weight_near_copy(0, False).start()
    for load in loads[7:]:
        load.start()
    edge_copy(0).wait_recv()
    normed[:EDGE] = norm_rows(edges[0])
    edge_copy(1).wait_recv()
    normed[ROWS + EDGE :] = norm_rows(edges[1])

    loads[2].wait()
    loads[3].wait()
    both = jnp.dot(normed[...], glu[...], preferred_element_type=F32)
    gated[...] = (both[:, :WIDTH] * jax.nn.sigmoid(both[:, WIDTH:])).astype(BF16).astype(F32)

    for side in range(2):
        weight_y_arrival(0, side).wait_recv()
        weight_x_copy(0, side).start()
        weight_x_copy(1, side).start()
    weight_near_copy(1, False).start()

    @pl.when(frame == 0)
    def _():
        gated[:EDGE] = jnp.zeros((EDGE, WIDTH), F32)

    @pl.when(frame == frame_count - 1)
    def _():
        gated[ROWS + EDGE :] = jnp.zeros((EDGE, WIDTH), F32)

    for load in loads[4:7]:
        load.wait()

    def share_rows(part, which):
        return pl.ds(pl.multiple_of(part * PART + SHARE * which, SHARE), SHARE)

    def swished_copy(part, index):
        flips = ((False, True), (True, False), (True, True))[index]
        return remote(
            swished.at[share_rows(part, core if index == 1 else 1 - core)],
            swished_all.at[part, own_head],
            swished_send_sem.at[part, index],
            swished_recv_sem.at[part, index],
            head_device(*flips),
        )

    def swished_arrival(part, index):
        head = (near_head, far_head, cross_head)[index]
        return remote(
            swished.at[share_rows(part, core)],
            swished_all.at[part, head],
            swished_send_sem.at[part, index],
            swished_recv_sem.at[part, index],
            head_device(False, True),
        )

    def normed_copy(part, arriving):
        block = normed_again.at[share_rows(part, 1 - core if arriving else core)]
        return remote(
            block,
            block,
            normed_send_sem.at[part],
            normed_recv_sem.at[part],
            head_device(False, True),
        )

    def residual_copy(part, arriving):
        return remote(
            residual_send.at[part],
            residual.at[share_rows(part, 1 - core if arriving else core)],
            residual_send_sem.at[part],
            residual_recv_sem.at[part],
            head_device(False, True),
        )

    def convolve(part):
        def piece(index, carry):
            lanes = pl.ds(pl.multiple_of(index * LANES, LANES), LANES)
            start = part * PART
            block = gated[pl.ds(start, PART + 2 * EDGE), lanes]
            taps = taps_ref[:, lanes]
            total = jnp.zeros((PART, LANES), F32)
            for shift in range(8):
                partial = jnp.zeros((PART + 8, LANES), F32)
                for step in range(4):
                    tap = 8 * step + shift - 1
                    if 0 <= tap < KW:
                        partial += taps[tap : tap + 1] * block[8 * step : 8 * step + PART + 8]
                total += partial[shift : shift + PART]
            shifted = total * scale_ref[:, lanes] + shift_ref[:, lanes]
            swished[pl.ds(start, PART), lanes] = (shifted * jax.nn.sigmoid(shifted)).astype(BF16)
            return carry

        lax.fori_loop(0, WIDTH // LANES, piece, 0)
        for index in (1, 2, 0):
            swished_copy(part, index).start()
        swished_all[part, own_head] = swished[share_rows(part, core)]

    def add_residual(part):
        for index in range(3):
            swished_arrival(part, index).wait_recv()
        rows = share_rows(part, core)
        whole = jnp.concatenate([swished_all[part, head] for head in range(4)], axis=1)
        sums[...] = frames[rows].astype(F32) + jnp.dot(
            whole, point_all[...], preferred_element_type=F32
        )
        normed_again[rows] = norm_rows(sums[...])
        normed_copy(part, False).start()
        residual[rows] = sums[:, columns_of(own_head)]
        residual_send[part] = sums[:, columns_of(near_head)]
        residual_copy(part, False).start()

    def kv_copy(part, index):
        return remote(
            kv_ref.at[part, index],
            kv_all.at[GROUP + slot, part, pl.ds(0, UNIT)],
            kv_send_sem.at[part, index],
            kv_recv_sem.at[part, slot],
            partner(index),
        )

    def kv_arrival(part, index):
        return remote(
            kv_ref.at[part, index],
            kv_all.at[GROUP + index, part, pl.ds(0, UNIT)],
            kv_send_sem.at[part, index],
            kv_recv_sem.at[part, index],
            partner(index),
        )

    def project(part):
        normed_copy(part, True).wait_recv()
        columns = pl.ds(part * PART, PART)
        turned = jnp.dot(
            normed_again[pl.ds(part * PART, PART)],
            key_value_weight[...],
            preferred_element_type=F32,
        ).T
        cosine, sine = rotation[0, :, columns], rotation[1, :, columns]
        for index in range(HEADS_HERE):
            base = index * HD
            first = turned[base : base + HALF_HD]
            second = turned[base + HALF_HD : base + HD]
            kv_ref[part, index, :HALF_HD] = (first * cosine - second * sine).astype(BF16)
            kv_ref[part, index, HALF_HD:HD] = (second * cosine + first * sine).astype(BF16)
            kv_ref[part, index, HD:] = turned[WIDTH + base : WIDTH + base + HD].astype(BF16)

    def send_pairs(part):
        for index in range(GROUP):

            @pl.when(jnp.logical_not(is_self(index)))
            def _():
                kv_copy(part, index).start()

            @pl.when(is_self(index))
            def _():
                kv_all[GROUP + slot, part, :UNIT] = kv_ref[part, index]

    def await_sent(copy, part):
        for index in range(GROUP):

            @pl.when(jnp.logical_not(is_self(index)))
            def _():
                copy(part, index).wait_send()

    for part in range(PARTS):
        convolve(part)

    for side in range(2):
        weight_y_arrival(1, side).wait_recv()
    weight_near_copy(2, False).start()
    for way in range(2):
        for side in range(2):
            weight_x_arrival(way, side).wait_recv()
        weight_near_copy(3 + way, False).start()

    loads[7].wait()
    lane = lax.broadcasted_iota(jnp.int32, (2, HALF_HD, LANES), 2)
    far = jnp.sum(
        jnp.where(lane == frame, angle[:, :, ROWS:], 0.0), axis=-1, keepdims=True
    )
    cosine, sine = angle[0, :, :ROWS], angle[1, :, :ROWS]
    rotation[0] = cosine * far[0] - sine * far[1]
    rotation[1] = sine * far[0] + cosine * far[1]
    for block in range(3 * GROUP):
        kv_all[block, :, UNIT:] = jnp.ones((PARTS, PADDED_UNIT - UNIT, PART), BF16)
    for load in loads[8:]:
        load.wait()

    for index in range(5):
        weight_near_copy(index, True).wait_recv()
    add_residual(0)
    for part in range(1, PARTS):
        add_residual(part)
        project(part - 1)
        if part <= 2:
            send_pairs(part - 1)
    project(PARTS - 1)

    turned_queries = (
        jnp.dot(normed_again[...], query_weight[...], preferred_element_type=F32) * SCALE
    ).T
    for index in range(HEADS_HERE):
        base = index * HD
        first = turned_queries[base : base + HALF_HD]
        second = turned_queries[base + HALF_HD : base + HD]
        cosine, sine = rotation[0], rotation[1]
        low = (first * cosine - second * sine).astype(BF16)
        high = (second * cosine + first * sine).astype(BF16)
        for chunk in range(CHUNKS):
            columns = slice(chunk * CHUNK, (chunk + 1) * CHUNK)
            q_ref[chunk, index, :HALF_HD] = low[:, columns]
            q_ref[chunk, index, HALF_HD:] = high[:, columns]

    def q_copy(chunk, index):
        return remote(
            q_ref.at[chunk, index],
            q_all.at[chunk, slot],
            q_send_sem.at[chunk, index],
            q_recv_sem.at[chunk, slot],
            partner(index),
        )

    def send_queries(chunk):
        for index in range(GROUP):

            @pl.when(jnp.logical_not(is_self(index)))
            def _():
                q_copy(chunk, index).start()

            @pl.when(is_self(index))
            def _():
                q_all[chunk, slot] = q_ref[chunk, index]

    def turn_keys(block, part):
        keys[block, pl.ds(part * PART, PART)] = kv_all[block, part, :HD].T

    def relay(part, index, upward):
        at = index if upward else 2 * GROUP + index
        flag = index if upward else GROUP + index
        return remote(
            kv_all.at[GROUP + index, part, pl.ds(0, UNIT)],
            kv_all.at[at, part, pl.ds(0, UNIT)],
            relay_send_sem.at[part, flag],
            relay_recv_sem.at[part, flag],
            group_device(1 if upward else -1),
        )

    for part in range(PARTS):
        await_sent(kv_copy, part)
        if part + 2 < PARTS:
            send_pairs(part + 2)
        else:
            send_queries(part + 2 - PARTS)
        for index in range(GROUP):

            @pl.when(jnp.logical_not(is_self(index)))
            def _():
                kv_arrival(part, index).wait_recv()

            relay(part, index, True).start()
            relay(part, index, False).start()
            turn_keys(GROUP + index, part)

    def relay_arrivals(near):
        low = core == (1 if near else 0)
        for part in range(PARTS):
            for index in range(GROUP):
                at = jnp.where(low, index, 2 * GROUP + index)
                flag = jnp.where(low, index, GROUP + index)
                remote(
                    kv_all.at[GROUP + index, part, pl.ds(0, UNIT)],
                    kv_all.at[at, part, pl.ds(0, UNIT)],
                    relay_send_sem.at[part, flag],
                    relay_recv_sem.at[part, flag],
                    group_device(1),
                ).wait_recv()
                turn_keys(at, part)

    relay_arrivals(True)

    def await_queries(chunk):
        for index in range(GROUP):

            @pl.when(jnp.logical_not(is_self(index)))
            def _():
                remote(
                    q_ref.at[chunk, index],
                    q_all.at[chunk, index],
                    q_send_sem.at[chunk, index],
                    q_recv_sem.at[chunk, index],
                    partner(index),
                ).wait_recv()

    def query_block(turn):
        return jnp.where(core == 1, turn, GROUP - 1 - turn)

    def key_block(turn, index):
        return jnp.where(core == 1, turn + index, 3 * GROUP - 1 - turn - index)

    def score(chunk, turn, first, last, target, buffer):
        turned = q_all[chunk, query_block(turn)]
        for index in range(first, last):
            target[buffer, index - first] = contract(
                keys[key_block(turn, index)], turned, 1, 0
            )

    def weigh(turn, first, last, source, buffer, largest, total):
        for index in range(first, last):
            weights = jnp.exp2(source[buffer, index - first] - largest).astype(BF16)
            block = key_block(turn, index)
            values = jnp.concatenate(
                [kv_all[block, part, HD:] for part in range(PARTS)], axis=1
            )
            total += contract(values, weights, 1, 0)
        return total

    def highest(source, buffer, count):
        return functools.reduce(
            jnp.maximum,
            [jnp.max(source[buffer, index], axis=0, keepdims=True) for index in range(count)],
        )

    def near_turn(chunk, turn, buffer):
        count = WINDOW - 1 - turn
        largest = highest(scores, buffer, count)
        peaks[chunk, turn, 0:1] = largest
        totals[chunk, turn] = weigh(
            turn, 0, count, scores, buffer, largest, jnp.zeros((HD + 16, CHUNK), F32)
        )

    def near_stage(chunk):
        score(chunk, 0, 0, WINDOW - 1, scores, 0)
        for turn in range(GROUP):
            if turn < GROUP - 1:
                score(chunk, turn + 1, 0, WINDOW - 2 - turn, scores, (turn + 1) % 2)
            near_turn(chunk, turn, turn % 2)

    def far_turn(chunk, turn, buffer):
        earlier = peaks[chunk, turn, 0:1]
        largest = jnp.maximum(earlier, highest(far_scores, buffer, turn + 1))
        total = weigh(
            turn,
            WINDOW - 1 - turn,
            WINDOW,
            far_scores,
            buffer,
            largest,
            totals[chunk, turn] * jnp.exp2(earlier - largest),
        )
        mixed[chunk, turn] = (total[:HD] / total[HD : HD + 1]).astype(BF16)

    def far_stage(chunk):
        score(chunk, 0, WINDOW - 1, WINDOW, far_scores, 0)
        for turn in range(GROUP):
            if turn < GROUP - 1:
                score(chunk, turn + 1, WINDOW - 2 - turn, WINDOW, far_scores, (turn + 1) % 2)
            far_turn(chunk, turn, turn % 2)

    def o_copy(chunk, turn):
        return remote(
            mixed.at[chunk, turn],
            gathered.at[chunk, slot],
            o_send_sem.at[chunk, turn],
            o_recv_sem.at[chunk, slot],
            partner(query_block(turn)),
        )

    def send_mixed(chunk):
        for turn in range(GROUP):

            @pl.when(is_self(query_block(turn)))
            def _():
                gathered[chunk, slot] = mixed[chunk, turn]

            @pl.when(jnp.logical_not(is_self(query_block(turn))))
            def _():
                o_copy(chunk, turn).start()

    def near_copy(chunk):
        return remote(
            near_send.at[chunk],
            near_recv.at[chunk],
            near_send_sem.at[chunk],
            near_recv_sem.at[chunk],
            head_device(False, True),
        )

    def far_copy(chunk):
        return remote(
            far_send.at[chunk],
            far_recv.at[chunk],
            far_send_sem.at[chunk],
            far_recv_sem.at[chunk],
            head_device(True, False),
        )

    def rows_of(chunk):
        return pl.ds(pl.multiple_of(chunk * CHUNK, CHUNK), CHUNK)

    def project_out(chunk):
        for index in range(GROUP):

            @pl.when(jnp.logical_not(is_self(index)))
            def _():
                remote(
                    mixed.at[chunk, index],
                    gathered.at[chunk, index],
                    o_send_sem.at[chunk, index],
                    o_recv_sem.at[chunk, index],
                    partner(index),
                ).wait_recv()

        turned = gathered[chunk].reshape(WIDTH, CHUNK).T
        terms[...] = jnp.dot(turned, weight_ref[...], preferred_element_type=F32)
        near_send[chunk, 0] = terms[:, columns_of(near_head)].astype(BF16)
        near_send[chunk, 1] = terms[:, columns_of(cross_head)].astype(BF16)
        near_copy(chunk).start()
        residual[rows_of(chunk)] += terms[:, columns_of(own_head)]
        far_own[chunk] = terms[:, columns_of(far_head)]

    def sum_out(chunk):
        near_copy(chunk).wait_recv()
        far_send[chunk] = (far_own[chunk] + near_recv[chunk, 1].astype(F32)).astype(BF16)
        far_copy(chunk).start()
        residual[rows_of(chunk)] += near_recv[chunk, 0].astype(F32)

    for part in range(PARTS):
        residual_copy(part, True).wait_recv()
    def early(chunk, carry):
        await_sent(q_copy, chunk)
        send_queries(chunk + 2)
        await_queries(chunk)
        near_stage(chunk)
        return carry

    lax.fori_loop(0, 2, early, 0)
    relay_arrivals(False)

    def finish(chunk, carry):
        far_stage(chunk)
        send_mixed(chunk)
        return carry

    lax.fori_loop(0, 2, finish, 0)

    def late(chunk, carry):
        await_queries(chunk)
        near_stage(chunk)
        project_out(chunk - 2)
        far_stage(chunk)
        send_mixed(chunk)
        sum_out(chunk - 2)
        return carry

    lax.fori_loop(2, CHUNKS, late, 0)
    for chunk in range(2, CHUNKS):
        project_out(chunk)
        sum_out(chunk)
    for chunk in range(CHUNKS):
        far_copy(chunk).wait_recv()
        rows = pl.ds(chunk * CHUNK, CHUNK)
        out_ref[rows] = (residual[rows] + far_recv[chunk].astype(F32)).astype(BF16)

    for index in range(GROUP):

        @pl.when(jnp.logical_not(is_self(index)))
        def _():
            for chunk in range(2, CHUNKS):
                q_copy(chunk, index).wait_send()

        for part in range(PARTS):
            relay(part, index, True).wait_send()
            relay(part, index, False).wait_send()
    for turn in range(GROUP):

        @pl.when(jnp.logical_not(is_self(query_block(turn))))
        def _():
            for chunk in range(CHUNKS):
                o_copy(chunk, turn).wait_send()

    edge_copy(0).wait_send()
    edge_copy(1).wait_send()
    for part in range(PARTS):
        normed_copy(part, False).wait_send()
        residual_copy(part, False).wait_send()
        for index in range(3):
            swished_copy(part, index).wait_send()
    for side in range(2):
        for turn in range(2):
            weight_y_copy(turn, side).wait_send()
            weight_x_copy(turn, side).wait_send()
    for index in range(5):
        weight_near_copy(index, False).wait_send()
    for chunk in range(CHUNKS):
        near_copy(chunk).wait_send()
        far_copy(chunk).wait_send()


def angle_table(frame_count):
    inverse = 10000.0 ** (-np.arange(HALF_HD) * (2.0 / HD))
    starts = np.zeros(LANES)
    starts[:frame_count] = np.arange(frame_count) * float(ROWS)
    angles = inverse[:, None] * np.concatenate([np.arange(ROWS), starts])[None, :]
    return jnp.asarray(np.stack([np.cos(angles), np.sin(angles)]).astype(np.float32))


def shards(
    frame_count,
    frames,
    glu_weight,
    depth_kernel,
    bn_scale,
    bn_shift,
    point_weight,
    qkv_weight,
    out_weight,
):
    vmem = pl.BlockSpec(memory_space=pltpu.VMEM)
    hbm = pl.BlockSpec(memory_space=pl.ANY)
    dma = pltpu.SemaphoreType.DMA
    space = pltpu.VMEM
    return pl.pallas_call(
        functools.partial(kernel, frame_count),
        out_shape=jax.ShapeDtypeStruct((ROWS, WIDTH), BF16),
        in_specs=[hbm] * 9,
        out_specs=vmem,
        scratch_shapes=[
            space((ROWS, D), BF16),
            space((D, 2 * WIDTH), BF16),
            space((D, D), BF16),
            space((D, 2 * WIDTH), BF16),
            space((D, WIDTH), BF16),
            space((WIDTH, D), BF16),
            space((2, HALF_HD, ROWS + LANES), F32),
            space((KW, WIDTH), F32),
            space((1, WIDTH), F32),
            space((1, WIDTH), F32),
            space((2, EDGE, D), BF16),
            space((ROWS + 2 * EDGE, D), BF16),
            space((ROWS + 2 * EDGE, WIDTH), F32),
            space((ROWS, WIDTH), BF16),
            space((PARTS, 4, SHARE, WIDTH), BF16),
            space((SHARE, D), F32),
            space((CHUNK, D), F32),
            space((ROWS, WIDTH), F32),
            space((PARTS, SHARE, WIDTH), F32),
            space((ROWS, D), BF16),
            space((2, HALF_HD, ROWS), F32),
            space((PARTS, GROUP, UNIT, PART), BF16),
            space((CHUNKS, GROUP, HD, CHUNK), BF16),
            space((3 * GROUP, PARTS, PADDED_UNIT, PART), BF16),
            space((3 * GROUP, ROWS, HD), BF16),
            space((CHUNKS, GROUP, HD, CHUNK), BF16),
            space((2, WINDOW - 1, ROWS, CHUNK), F32),
            space((2, GROUP, ROWS, CHUNK), F32),
            space((CHUNKS, GROUP, 8, CHUNK), F32),
            space((CHUNKS, GROUP, HD + 16, CHUNK), F32),
            space((CHUNKS, GROUP, HD, CHUNK), BF16),
            space((CHUNKS, GROUP, HD, CHUNK), BF16),
            space((CHUNKS, 2, CHUNK, WIDTH), BF16),
            space((CHUNKS, 2, CHUNK, WIDTH), BF16),
            space((CHUNKS, CHUNK, WIDTH), F32),
            space((CHUNKS, CHUNK, WIDTH), BF16),
            space((CHUNKS, CHUNK, WIDTH), BF16),
            dma((12,)),
            dma((2,)),
            dma((2,)),
            dma((2, 2)),
            dma((2, 2)),
            dma((2, 2)),
            dma((2, 2)),
            dma((5,)),
            dma((5,)),
            dma((PARTS, 3)),
            dma((PARTS, 3)),
            dma((PARTS,)),
            dma((PARTS,)),
            dma((PARTS,)),
            dma((PARTS,)),
            dma((PARTS, GROUP)),
            dma((PARTS, GROUP)),
            dma((CHUNKS, GROUP)),
            dma((CHUNKS, GROUP)),
            dma((PARTS, 2 * GROUP)),
            dma((PARTS, 2 * GROUP)),
            dma((CHUNKS, GROUP)),
            dma((CHUNKS, GROUP)),
            dma((CHUNKS,)),
            dma((CHUNKS,)),
            dma((CHUNKS,)),
            dma((CHUNKS,)),
        ],
        compiler_params=pltpu.CompilerParams(
            collective_id=1, has_side_effects=True, vmem_limit_bytes=60 << 20
        ),
    )(
        frames,
        glu_weight,
        depth_kernel,
        bn_scale,
        bn_shift,
        point_weight,
        qkv_weight,
        out_weight,
        angle_table(frame_count),
    )


def solution(mesh):
    return jax.shard_map(
        functools.partial(shards, mesh.shape["frame"]),
        mesh=mesh,
        in_specs=(
            P("frame", None),
            P(None, None, "head"),
            P(None, "head"),
            P("head"),
            P("head"),
            P("head", None),
            P(None, None, "head"),
            P("head", None),
        ),
        out_specs=P("frame", "head"),
        check_vma=False,
    )
```

profile of v0, /device:TPU:16, one launch (start us, length us, event | category | flops | bytes accessed | tf_op | source)
XLA Modules:
  0.0 82.2 jit_solution(6889789132771485872)
XLA Ops:
  0.0 80.4 %shard_map.91 = bf16[512,384]{1,0:T(8,128)(2,1)} custom-call(bf16[512,1536]{1,0:T(8,128)(2,1)} %frames_hbm.1, bf16[2,1536,384]{2,1,0:T(8,128)(2,1)} %glu_hbm.1, f32[31,384]{1,0:T(8,128)} %depth_hbm.1, f32[384]{0:T(512)} %scale_hbm.1, f32[384]{0:T(512)} %shift_hbm.1, bf16[384,1536]{1,0:T(8,128)(2,1)} %point_hbm.1, bf16[3,1536,384]{2,1,0:T(8,128)(2,1)} %qkv_hbm.1, ...), custom_call_target="tpu_custom_call" | custom-call | tf_op jit(solution)/shard_map/pallas_call | solution.py:860
  80.4 1.8 %copy.11 = bf16[512,384]{1,0:T(8,128)(2,1)} copy(bf16[512,384]{1,0:T(8,128)(2,1)} %shard_map.91) | data formatting | bytes 786432
where the time goes:
time: 82.3 us; the launch traced here: 82.2 us
  Pallas kernels  80.4 us (98%)
  local copies, waits for them, and re-layouts  1.78 us (2%)
    pallas_call x1, Pallas kernels, shards(): pl.pallas_call(functools.partial(kernel, frame_count), out_shape=jax.Shap...  80.4 us
    unnamed x1, local copies, waits for them, and re-layouts  1.78 us

commit v1 on v0

--- a/solution.py
+++ b/solution.py
@@ -694,6 +694,21 @@
                 score(chunk, turn + 1, WINDOW - 2 - turn, WINDOW, far_scores, (turn + 1) % 2)
             far_turn(chunk, turn, turn % 2)
 
+    def whole_turn(chunk, turn):
+        if turn < GROUP - 1:
+            score(chunk, turn + 1, 0, WINDOW, scores, (turn + 1) % 2)
+        buffer = turn % 2
+        total = weigh(
+            turn,
+            0,
+            WINDOW,
+            scores,
+            buffer,
+            highest(scores, buffer, WINDOW),
+            jnp.zeros((HD + 16, CHUNK), F32),
+        )
+        mixed[chunk, turn] = (total[:HD] / total[HD : HD + 1]).astype(BF16)
+
     def o_copy(chunk, turn):
         return remote(
             mixed.at[chunk, turn],
@@ -703,8 +718,8 @@
             partner(query_block(turn)),
         )
 
-    def send_mixed(chunk):
-        for turn in range(GROUP):
+    def send_mixed(chunk, turns):
+        for turn in turns:
 
             @pl.when(is_self(query_block(turn)))
             def _():
@@ -776,17 +791,21 @@
 
     def finish(chunk, carry):
         far_stage(chunk)
-        send_mixed(chunk)
+        send_mixed(chunk, range(GROUP))
         return carry
 
     lax.fori_loop(0, 2, finish, 0)
 
     def late(chunk, carry):
         await_queries(chunk)
-        near_stage(chunk)
+        score(chunk, 0, 0, WINDOW, scores, 0)
+        whole_turn(chunk, 0)
+        whole_turn(chunk, 1)
+        send_mixed(chunk, (0, 1))
         project_out(chunk - 2)
-        far_stage(chunk)
-        send_mixed(chunk)
+        whole_turn(chunk, 2)
+        whole_turn(chunk, 3)
+        send_mixed(chunk, (2, 3))
         sum_out(chunk - 2)
         return carry
 
@@ -794,10 +813,13 @@
     for chunk in range(2, CHUNKS):
         project_out(chunk)
         sum_out(chunk)
-    for chunk in range(CHUNKS):
+    def finish_rows(chunk):
         far_copy(chunk).wait_recv()
         rows = pl.ds(chunk * CHUNK, CHUNK)
         out_ref[rows] = (residual[rows] + far_recv[chunk].astype(F32)).astype(BF16)
+
+    for chunk in range(CHUNKS - 2):
+        finish_rows(chunk)
 
     for index in range(GROUP):
 
@@ -829,6 +851,8 @@
             weight_x_copy(turn, side).wait_send()
     for index in range(5):
         weight_near_copy(index, False).wait_send()
+    for chunk in range(CHUNKS - 2, CHUNKS):
+        finish_rows(chunk)
     for chunk in range(CHUNKS):
         near_copy(chunk).wait_send()
         far_copy(chunk).wait_send()
@@ -889,7 +913,7 @@
             space((3 * GROUP, PARTS, PADDED_UNIT, PART), BF16),
             space((3 * GROUP, ROWS, HD), BF16),
             space((CHUNKS, GROUP, HD, CHUNK), BF16),
-            space((2, WINDOW - 1, ROWS, CHUNK), F32),
+            space((2, WINDOW, ROWS, CHUNK), F32),
             space((2, GROUP, ROWS, CHUNK), F32),
             space((CHUNKS, GROUP, 8, CHUNK), F32),
             space((CHUNKS, GROUP, HD + 16, CHUNK), F32),

time: 82.3 us -> 82.2 us (level)
  no operation moved by 1% of the time
where the time goes in v1:
time: 82.2 us; the launch traced here: 82 us
  Pallas kernels  80.2 us (98%)
  local copies, waits for them, and re-layouts  1.78 us (2%)
    pallas_call x1, Pallas kernels, shards(): pl.pallas_call(functools.partial(kernel, frame_count), out_shape=jax.Shap...  80.2 us
    unnamed x1, local copies, waits for them, and re-layouts  1.78 us

profile of v1, /device:TPU:16, one launch (start us, length us, event | category | flops | bytes accessed | tf_op | source)
XLA Modules:
  0.0 82.0 jit_solution(9949998572818260244)
XLA Ops:
  0.0 80.2 %shard_map.91 = bf16[512,384]{1,0:T(8,128)(2,1)} custom-call(bf16[512,1536]{1,0:T(8,128)(2,1)} %frames_hbm.1, bf16[2,1536,384]{2,1,0:T(8,128)(2,1)} %glu_hbm.1, f32[31,384]{1,0:T(8,128)} %depth_hbm.1, f32[384]{0:T(512)} %scale_hbm.1, f32[384]{0:T(512)} %shift_hbm.1, bf16[384,1536]{1,0:T(8,128)(2,1)} %point_hbm.1, bf16[3,1536,384]{2,1,0:T(8,128)(2,1)} %qkv_hbm.1, ...), custom_call_target="tpu_custom_call" | custom-call | tf_op jit(solution)/shard_map/pallas_call | solution.py:884
  80.3 1.8 %copy.11 = bf16[512,384]{1,0:T(8,128)(2,1)} copy(bf16[512,384]{1,0:T(8,128)(2,1)} %shard_map.91) | data formatting | bytes 786432
